TPU v7x, 512 devices: a whole 4x4x16 slice. The times are simulated.
512 devices in a mesh: dp: 32 (over x, y, core), seq: 16 (over z).
Axes of the slice: x: 4, y: 4, z: 16, core: 2. Of those that a mesh axis runs over, the one named last changes fastest.
Arguments:
- tile_tokens: bfloat16 [32, 512, 3200], P('dp', 'seq'), may hold values from -6 to 6
- proj_weight: bfloat16 [3200, 8192], P('dp', 'seq')
- text_hidden: bfloat16 [32, 2048, 8192], P('dp', 'seq'), may hold values from -6 to 6
- cotangent: bfloat16 [32, 2048, 8192], P('dp', 'seq'), may hold values from -1.1953125 to 1.1953125
- norm_gain: float32 [8192], replicated, may hold values from 0.25 to 1.75
- placeholders: int32 [32, 512], P('dp'), may hold values from 0 to 2047, as said below
- bucket_levels: int32 [32, 16, 3200], P('dp', 'seq'), may hold values from 2 to 16
- row_draws: float32 [32, 16, 3200], P('dp', 'seq'), may hold values from 0 to 1
- column_draws: float32 [32, 8192], P('dp', 'seq'), may hold values from 0 to 1
Outputs:
- weight_grad: float32 [3200, 8192], P('dp', 'seq')
- gain_grad: float32 [8192], replicated
Inputs may be any that keep to these rules, and one draw needn't show every extreme that they name: Each row is strictly increasing. Among the positions of one device's block of 128 positions stand at most 48 placeholders, and in every row some block holds exactly 48.
All inputs are finite; a program needn't handle non-finite values.
Results may differ from a plain program's by a relative error of at most 0.014.
Values may be sent and summed in bfloat16 or wider, within the bound.
A program may use at most 64 MiB of HBM per device.

v0:
```python
import jax
import jax.numpy as jnp
from jax import lax
from jax.sharding import Mesh
from jax.sharding import PartitionSpec as P

IMG_MOST = 48
DP = ("dp_0", "dp_1", "dp_2")
DP_SEQ = ("dp_0", "dp_1", "dp_2", "seq")
EPSILON = 1e-06


def copy_for_each(value, axis):
    copies = jnp.broadcast_to(value, (lax.axis_size(axis), *value.shape))
    return lax.all_to_all(copies, axis, split_axis=0, concat_axis=0, tiled=True)


def of_everyone(value, axis):
    everything = copy_for_each(value, axis)
    return jnp.sum(everything, axis=0)


def in_one(arrays, axis):
    ravelled, at, outs = (jnp.concatenate([a.reshape(-1) for a in arrays]), 0, [])
    so_far = of_everyone(ravelled, axis)
    for a in arrays:
        outs.append(so_far[at : at + a.size].reshape(a.shape))
        at += a.size
    return tuple(outs)


def one_axis_at_a_time(value, axes):
    for axis in axes:
        value = lax.psum(value, axis)
    return value


def quantize(gradient, levels_now, rows_now, columns_now):
    bucket_norm = jnp.sqrt(jnp.sum(gradient * gradient, axis=1, keepdims=True) + EPSILON)
    step_count = levels_now.astype(jnp.float32)[:, None]
    offset = 0.25 + 0.25 * (rows_now[:, None] + columns_now[None, :])
    ratio = jnp.abs(gradient) / bucket_norm * step_count
    lower = jnp.floor(ratio)
    quantum = lower + jnp.clip(2.0 * (ratio - lower - offset) + 0.5, 0.0, 1.0)
    return jnp.sign(gradient) * bucket_norm * quantum / step_count


def on_device(
    tile_tokens,
    proj_weight,
    text_hidden,
    cotangent,
    norm_gain,
    placeholders,
    bucket_levels,
    row_draws,
    column_draws,
):
    seq_count = lax.axis_size("seq")
    seq_index = lax.axis_index("seq")
    replicas = lax.axis_size(DP)
    places = placeholders[0]
    image_total = places.shape[0]
    tok_rows = text_hidden.shape[1]
    model_width = text_hidden.shape[2]
    columns = proj_weight.shape[1]
    all_positions = tok_rows * seq_count
    zero_half = jnp.zeros((), jnp.bfloat16)
    own_text = text_hidden[0]
    own_cot = cotangent[0]
    gathered = lax.all_gather(tile_tokens[0], "seq", axis=0, tiled=True)
    patch_block = gathered
    embedded = jnp.dot(
        patch_block,
        lax.all_gather(proj_weight, DP, axis=0, tiled=True),
        preferred_element_type=jnp.float32,
    ).astype(jnp.bfloat16)
    image_marks = jnp.zeros((all_positions,), jnp.int32).at[places].set(1)
    local_marks = lax.dynamic_slice_in_dim(image_marks, seq_index * tok_rows, tok_rows)
    is_image = local_marks[:, None] == 1
    owners = places // tok_rows
    owner_ids = jnp.arange(seq_count, dtype=jnp.int32)
    counts = jnp.sum((owners[:, None] == owner_ids[None, :]).astype(jnp.int32), axis=0)
    starts = jnp.cumsum(counts) - counts
    own_start = starts[seq_index]
    own_count = counts[seq_index]
    slot_ids = jnp.arange(IMG_MOST, dtype=jnp.int32)
    source_rows = jnp.clip(own_start + slot_ids, 0, image_total - 1)
    local_slots = jnp.clip(jnp.take(places, source_rows) - seq_index * tok_rows, 0, tok_rows - 1)
    slot_live = (slot_ids < own_count)[:, None]
    flat_index = owners * IMG_MOST + (
        jnp.arange(image_total, dtype=jnp.int32) - jnp.take(starts, owners)
    )
    outgoing = jnp.where(slot_live, jnp.take(own_cot, local_slots, axis=0), zero_half)
    returned = lax.all_to_all(outgoing[None], "seq", split_axis=2, concat_axis=0, tiled=True)
    image_cot = jnp.take(returned.reshape(-1, columns), flat_index, axis=0).astype(jnp.float32)
    emb_float = embedded.astype(jnp.float32)
    column_gain = lax.dynamic_slice_in_dim(norm_gain, seq_index * columns, columns)
    grad_in = image_cot * column_gain[None, :]
    squares, mixed = in_one(
        (jnp.sum(emb_float * emb_float, axis=1), jnp.sum(grad_in * emb_float, axis=1)), "seq"
    )
    inverse = lax.rsqrt(squares / model_width + EPSILON)[:, None]
    normed = emb_float * inverse
    emb_grad = ((grad_in - normed * (mixed[:, None] * inverse / model_width)) * inverse).astype(
        jnp.bfloat16
    )
    image_part = jnp.sum(image_cot * normed, axis=0)
    text_float = own_text.astype(jnp.float32)
    text_inverse = lax.rsqrt(jnp.mean(text_float * text_float, axis=1, keepdims=True) + EPSILON)
    text_terms = own_cot.astype(jnp.float32) * text_float * text_inverse
    text_part = jnp.sum(jnp.where(is_image, 0.0, text_terms), axis=0)
    placed_part = lax.dynamic_update_slice_in_dim(
        jnp.zeros((model_width,), jnp.float32), image_part, seq_index * columns, 0
    )
    gain_part = text_part + placed_part
    own_levels = bucket_levels[0, 0]
    own_row_draws = row_draws[0, 0]
    own_column_draws = column_draws[0]
    patch_block = gathered
    gradient = lax.dot_general(
        patch_block, emb_grad, (((0,), (0,)), ((), ())), preferred_element_type=jnp.float32
    )
    summed = lax.psum_scatter(
        quantize(gradient, own_levels, own_row_draws, own_column_draws).astype(jnp.bfloat16),
        DP,
        scatter_dimension=0,
        tiled=True,
    ).astype(jnp.float32)
    gain_total = one_axis_at_a_time(gain_part, DP_SEQ)
    return (summed / replicas, gain_total / replicas)


def solution(mesh):
    finer = Mesh(mesh.devices.reshape(4, 4, 2, mesh.shape["seq"]), ("dp_0", "dp_1", "dp_2", "seq"))
    return jax.shard_map(
        on_device,
        mesh=finer,
        in_specs=(
            P(DP, "seq", None),
            P(DP, "seq"),
            P(DP, "seq", None),
            P(DP, "seq", None),
            P(),
            P(DP, None),
            P(DP, "seq", None),
            P(DP, "seq", None),
            P(DP, "seq"),
        ),
        out_specs=(P(DP, "seq"), P()),
        check_vma=False,
    )
```

profile of v0, /device:TPU:6, one launch (start us, length us, event | category | flops | bytes accessed | tf_op | source)
XLA Modules:
  0.0 358.7 jit_solution(13340607720197606231)
XLA Ops:
  7.2 0.7 all-gather.7.cloned.1.call-update
  7.9 0.7 all-gather.5.cloned.1.call-update
  8.6 0.7 add_select_fusion
  9.7 0.6 dynamic_slice.12
  10.3 0.7 fusion.39
  11.1 0.7 fusion.37
  11.8 1.5 gather_fusion
  13.2 0.7 fusion.36
  13.9 3.6 %gather_fusion.1 = bf16[48,8192]{1,0:T(8,128)(2,1)S(1)} fusion(bf16[128,8192]{1,0:T(8,128)(2,1)} %bitcast.91, s32[1024]{0:T(1024)S(1)} %pad_clamp_fusion.1), kind=kCustom, calls=%fused_computation.1 | custom fusion | bytes 1573056 | tf_op jit(solution)/shard_map/jit(_take)/gather | solution.py:94
  17.6 1.3 compare_and_fusion
  18.9 0.2 fusion.25
  19.0 6.8 %copy.37 = bf16[1,48,8192]{1,0,2:T(2,128)(2,1)} copy(bf16[1,48,8192]{2,1,0:T(8,128)(2,1)S(1)} %fusion.25) | data formatting | bytes 1572864 | tf_op jit(solution)/shard_map/jit(_where)/select_n | solution.py:94
  25.9 0.5 broadcast.663
  26.4 45.1 %reduce.24 = bf16[8192,48]{1,0:T(8,128)(2,1)S(1)} reduce(bf16[8192,1,48]{2,1,0:T(2,128)(2,1)} %bitcast.93, bf16[]{:T(256)} %broadcast.663), dimensions={1}, to_apply=%bitcast.79.reduce_sub_computation | reduce | bytes 1572866
  71.5 3.9 %reshape.481 = bf16[16,2,12288]{2,1,0:T(2,128)(2,1)} reshape(bf16[8192,48]{1,0:T(8,128)(2,1)S(1)} %reduce.24) | data formatting | bytes 1572864
  75.4 15.2 %all-to-all-start = ((bf16[16,2,12288]{2,1,0:T(2,128)(2,1)}), bf16[16,2,12288]{2,1,0:T(2,128)(2,1)S(1)}, u32[]{:S(2)}, u32[]{:S(2)}) async-start(bf16[16,2,12288]{2,1,0:T(2,128)(2,1)} %reshape.481), calls=%async_computation | async-start | bytes 1572864 | tf_op jit(solution)/shard_map/all_to_all | solution.py:95
  90.6 0.8 dynamic_slice.14
  91.4 4.3 %compare_select_fusion.2 = (s32[512,1]{0,1:T(1,128)S(1)}, s32[512,1]{0,1:T(1,128)S(1)}, s32[512,1]{0,1:T(1,128)S(1)}, s32[512,1]{0,1:T(1,128)S(1)}) fusion(s32[]{:T(128)} %bitcast.12, s32[]{:T(128)} %bitcast.13, s32[]{:T(128)} %bitcast.14, s32[]{:T(128)} %bitcast.15, s32[]{:T(128)} %bitcast.16, s32[]{:T(128)} %bitcast.18, s32[]{:T(128)} %bitcast.17, ...), kind=kLoop, calls=%fused_computation.62 | loop fusion | flops 16384 | bytes 10268 | tf_op jit(solution)/shard_map/jit(_take)/gather | solution.py:92
  95.8 5.8 %compare_and_fusion.1 = (pred[512]{0:T(512)(128)(4,1)S(1)}, s32[512]{0:T(512)S(1)}) fusion(pred[512]{0:T(512)(128)(4,1)S(1)} %get-tuple-element.24, pred[512]{0:T(512)(128)(4,1)S(1)} %get-tuple-element.22, pred[512]{0:T(512)(128)(4,1)S(1)} %get-tuple-element.23, pred[512]{0:T(512)(128)(4,1)S(1)} %get-tuple-element.21, ...), kind=kLoop, calls=%fused_computation.102 | loop fusion | flops 20480 | bytes 11300 | tf_op jit(solution)/shard_map/jit(_take)/and | solution.py:96
  101.6 36.3 %all-to-all-done = bf16[16,2,12288]{2,1,0:T(2,128)(2,1)S(1)} async-done(((bf16[16,2,12288]{2,1,0:T(2,128)(2,1)}), bf16[16,2,12288]{2,1,0:T(2,128)(2,1)S(1)}, u32[]{:S(2)}, u32[]{:S(2)}) %all-to-all-start) | async-done | bytes 786464 | tf_op jit(solution)/shard_map/all_to_all | solution.py:95
  137.9 7.9 %reshape.482 = bf16[8192,1,48]{2,1,0:T(2,128)(2,1)} reshape(bf16[16,2,12288]{2,1,0:T(2,128)(2,1)S(1)} %all-to-all-done) | data formatting | bytes 1572864
  145.8 8.1 %copy.38 = bf16[1,48,8192]{2,1,0:T(8,128)(2,1)S(1)} copy(bf16[1,48,8192]{1,0,2:T(2,128)(2,1)} %bitcast.94) | data formatting | bytes 1572864 | tf_op jit(solution)/shard_map/all_to_all | solution.py:95
  154.0 0.2 copy.48
  154.3 0.4 copy.39
  154.7 2.0 gather_fusion.2
  156.7 1.0 copy.40
  157.7 3.7 %reshape.455 = bf16[3200,512]{1,0:T(8,128)(2,1)S(1)} reshape(bf16[32,100,512]{2,1,0:T(8,128)(2,1)} %all-gather.7.cloned.1.call-done) | data formatting | bytes 6553600
  161.5 19.4 %all-gather.5.cloned.1.call-done = bf16[1,512,3200]{2,1,0:T(8,128)(2,1)} async-done(((bf16[1,32,3200]{2,1,0:T(8,128)(2,1)}), bf16[1,512,3200]{2,1,0:T(8,128)(2,1)}) %all-gather.5.cloned.1.call-update) | async-done | bytes 3276816 | tf_op jit(solution)/shard_map/all_gather | solution.py:71
  180.8 4.9 %fusion.23 = (f32[512]{0:T(512)S(1)}, f32[512]{0:T(512)S(1)}, bf16[512,512]{0,1:T(8,128)(2,1)}) fusion(f32[512]{0:T(512)S(1)} %dynamic_slice.14, bf16[512,512]{0,1:T(8,128)(2,1)} %copy.40, pred[512]{0:T(512)(128)(4,1)S(1)} %get-tuple-element.25, bf16[3200,512]{1,0:T(8,128)(2,1)S(1)} %reshape.455, bf16[1,512,3200]{2,1,0:T(8,128)(2,1)} %all-gather.5.cloned.1.call-done), kind=kOutput, calls=%fused_computation.35 | convolution fusion | flops 1680079872 | bytes 7608832 | tf_op jit(solution)/shard_map/dot_general | solution.py:73
  185.7 0.7 broadcast_in_dim.90
  186.4 6.6 %all-to-all-start.1 = ((f32[16,1,1024]{2,1,0:T(1,128)}), f32[16,1,1024]{2,1,0:T(1,128)S(1)}, u32[]{:S(2)}, u32[]{:S(2)}) async-start(f32[16,1,1024]{2,1,0:T(1,128)} %broadcast_in_dim.90), calls=%async_computation.1 | async-start | bytes 131072 | tf_op jit(solution)/shard_map/all_to_all | solution.py:15
  193.1 2.7 scatter_custom_fusion
  195.8 10.0 %all-to-all-done.1 = f32[16,1,1024]{2,1,0:T(1,128)S(1)} async-done(((f32[16,1,1024]{2,1,0:T(1,128)}), f32[16,1,1024]{2,1,0:T(1,128)S(1)}, u32[]{:S(2)}, u32[]{:S(2)}) %all-to-all-start.1) | async-done | bytes 65568 | tf_op jit(solution)/shard_map/all_to_all | solution.py:15
  205.9 4.4 %multiply_reduce_fusion = (f32[3200]{0:T(1024)S(1)}, f32[512,3200]{1,0:T(8,128)S(1)}) fusion(bf16[1,512,3200]{2,1,0:T(8,128)(2,1)} %all-gather.5.cloned.1.call-done, bf16[512,512]{0,1:T(8,128)(2,1)} %get-tuple-element.50, f32[512]{0:T(512)S(1)} %get-tuple-element.31, f32[512]{0:T(512)S(1)} %get-tuple-element.30, f32[512]{0:T(512)S(1)} %dynamic_slice.14, ...), kind=kOutput, calls=%fused_computation.12 | convolution fusion | flops 1683354496 | bytes 10898432 | tf_op jit(solution)/shard_map/dot_general | solution.py:121
  210.3 6.5 %fusion.6 = bf16[3200,512]{0,1:T(8,128)(2,1)} fusion(f32[512,3200]{1,0:T(8,128)S(1)} %get-tuple-element.52, f32[3200]{0:T(1024)S(1)} %convert_reduce_fusion.1, f32[512]{0:T(512)S(1)} %bitcast.103, f32[3200]{0:T(1024)S(1)} %reduce.13, f32[3200]{0:T(1024)S(1)} %add_sqrt_fusion), kind=kLoop, calls=%fused_computation.13 | loop fusion | flops 29491200 | bytes 9870848 | tf_op jit(solution)/shard_map/convert_element_type | solution.py:125
  216.9 1.4 dynamic-slice.1
  218.9 2.1 fusion.10
  221.0 2.5 fusion.9
  223.5 0.3 fusion.22
  223.8 0.2 add_dynamic-update-slice_fusion
  224.0 14.2 %psum.28 = f32[8192]{0:T(1024)S(1)} all-reduce(f32[8192]{0:T(1024)S(1)} %add_dynamic-update-slice_fusion), channel_id=1, replica_groups=mesh['dp_0'=4,'dp_1'=4,'dp_2'=2,'seq'=16] {'dp_0'}, use_global_device_ids=true, to_apply=%region_11.12 | all-reduce | flops 8192 | bytes 65536 | tf_op jit(solution)/shard_map/psum | solution.py:34
  238.2 17.1 %psum.29 = f32[8192]{0:T(1024)S(1)} all-reduce(f32[8192]{0:T(1024)S(1)} %psum.28), channel_id=1, replica_groups=mesh['dp_0'=4,'dp_1'=4,'dp_2'=2,'seq'=16] {'dp_1'}, use_global_device_ids=true, to_apply=%region_12.13 | all-reduce | flops 8192 | bytes 65536 | tf_op jit(solution)/shard_map/psum | solution.py:34
  255.3 3.4 psum.30
  258.7 54.0 %psum.31 = f32[8192]{0:T(1024)S(1)} all-reduce(f32[8192]{0:T(1024)S(1)} %psum.30), channel_id=1, replica_groups=mesh['dp_0'=4,'dp_1'=4,'dp_2'=2,'seq'=16] {'seq'}, use_global_device_ids=true, to_apply=%region_14.15 | all-reduce | flops 8192 | bytes 65536 | tf_op jit(solution)/shard_map/psum | solution.py:34
  312.7 0.6 broadcast_multiply_fusion
  313.3 37.0 %all-reduce.3.cloned.1.call-done = bf16[3200,512]{0,1:T(8,128)(2,1)} async-done(((bf16[3200,512]{0,1:T(8,128)(2,1)}), bf16[3200,512]{0,1:T(8,128)(2,1)}) %all-reduce.3.cloned.1.call-update) | async-done | bytes 3276816
  350.3 1.1 convert_multiply_fusion.7
  351.4 0.8 copy.42
  (39 shorter events, 0.9 us)
Async XLA Ops:
  7.2 150.5 %all-gather.7.cloned.1.call-start = ((), (), s32[]{:S(2)}) async-start(), calls=%async_computation.3 | async-start | bytes 3514368 | tf_op jit(solution)/shard_map/all_gather | solution.py:75
  7.9 172.9 %all-gather.5.cloned.1.call-start = ((), (), s32[]{:S(2)}) async-start(), calls=%async_computation.2 | async-start | bytes 3481600 | tf_op jit(solution)/shard_map/all_gather | solution.py:71
  26.4 65.0 %copy-start = (s32[1,512]{1,0:T(1,128)S(1)}, s32[1,512]{1,0:T(1,128)}, u32[]{:S(2)}) copy-start(s32[1,512]{1,0:T(1,128)} %param.14) | copy-start | bytes 6148
  75.4 62.5 %all-to-all-start = ((bf16[16,2,12288]{2,1,0:T(2,128)(2,1)}), bf16[16,2,12288]{2,1,0:T(2,128)(2,1)S(1)}, u32[]{:S(2)}, u32[]{:S(2)}) async-start(bf16[16,2,12288]{2,1,0:T(2,128)(2,1)} %reshape.481), calls=%async_computation | async-start | bytes 1572864 | tf_op jit(solution)/shard_map/all_to_all | solution.py:95
  180.8 12.2 %copy-start.5 = (f32[1,1,3200]{2,1,0:T(1,128)S(1)}, f32[1,1,3200]{2,1,0:T(1,128)}, u32[]{:S(2)}) copy-start(f32[1,1,3200]{2,1,0:T(1,128)} %param.16) | copy-start | bytes 38404
  180.8 14.9 %copy-start.4 = (s32[1,1,3200]{2,1,0:T(1,128)S(1)}, s32[1,1,3200]{2,1,0:T(1,128)}, u32[]{:S(2)}) copy-start(s32[1,1,3200]{2,1,0:T(1,128)} %param.15) | copy-start | bytes 38404
  186.4 19.4 %all-to-all-start.1 = ((f32[16,1,1024]{2,1,0:T(1,128)}), f32[16,1,1024]{2,1,0:T(1,128)S(1)}, u32[]{:S(2)}, u32[]{:S(2)}) async-start(f32[16,1,1024]{2,1,0:T(1,128)} %broadcast_in_dim.90), calls=%async_computation.1 | async-start | bytes 131072 | tf_op jit(solution)/shard_map/all_to_all | solution.py:15
  193.0 157.3 %all-reduce.3.cloned.1.call-start = ((), (), s32[]{:S(2)}) async-start(), calls=%async_computation.4 | async-start | bytes 6553600
  205.9 4.4 %copy-start.6 = (f32[1,512]{1,0:T(1,128)S(1)}, f32[1,512]{1,0:T(1,128)}, u32[]{:S(2)}) copy-start(f32[1,512]{1,0:T(1,128)} %param.17) | copy-start | bytes 6148
  216.8 4.3 %copy-start.1 = (bf16[1,128,8192]{2,1,0:T(8,128)(2,1)S(1)}, bf16[1,128,8192]{2,1,0:T(8,128)(2,1)}, u32[]{:S(2)}) copy-start(bf16[1,128,8192]{2,1,0:T(8,128)(2,1)} %param.12) | copy-start | bytes 6291460
  216.8 6.8 %copy-start.2 = (bf16[512,512]{0,1:T(8,128)(2,1)S(1)}, bf16[512,512]{0,1:T(8,128)(2,1)}, u32[]{:S(2)}) copy-start(bf16[512,512]{0,1:T(8,128)(2,1)} %copy.40) | copy-start | bytes 1572868
  216.8 6.8 %copy-start.3 = (bf16[512,512]{0,1:T(8,128)(2,1)S(1)}, bf16[512,512]{0,1:T(8,128)(2,1)}, u32[]{:S(2)}) copy-start(bf16[512,512]{0,1:T(8,128)(2,1)} %get-tuple-element.50) | copy-start | bytes 1572868
Sparse Core Ops, SparseCore 0:
  11.1 64.6 all-gather.6
  77.9 102.9 all-gather.4
  216.9 133.3 all-reduce.2
where the time goes:
time: 360 us; the launch traced here: 359 us
  waiting for transfers between devices  104 us (29%)
  blocking collectives  88.7 us (25%)
  other arithmetic  72.6 us (20%)
  local copies, waits for them, and re-layouts  47.6 us (13%)
  starting transfers between devices  21.9 us (6%)
  between operations  14.7 us (4%)
  matrix products  9.27 us (3%)
    psum x4, blocking collectives, one_axis_at_a_time(): value = lax.psum(value, axis)  88.7 us
    unnamed x2, other arithmetic  45.2 us
    unnamed x4, waiting for transfers between devices  38.4 us
    all_to_all x1, waiting for transfers between devices, on_device(): lax.all_to_all(outgoing[None], 'seq', split_axis=2, concat_axis=0, tiled=...  36.3 us
    all_gather x1, waiting for transfers between devices, on_device(): gathered = lax.all_gather(tile_tokens[0], 'seq', axis=0, tiled=True)  19.4 us
    unnamed x21, local copies, waits for them, and re-layouts  18.5 us
    all_to_all x1, starting transfers between devices, on_device(): lax.all_to_all(outgoing[None], 'seq', split_axis=2, concat_axis=0, tiled=...  15.2 us
    all_to_all x1, waiting for transfers between devices, copy_for_each(): return lax.all_to_all(copies, axis, split_axis=0, concat_axis=0, tiled=True)  9.99 us
  transfers between devices with their start and end apart: 5, of which 4 were waited for; matrix products, arithmetic and copies ran while one was open for 31% of the time, Pallas kernels for 0%

commit v1 on v0

--- a/solution.py
+++ b/solution.py
@@ -8,6 +8,12 @@
 DP = ("dp_0", "dp_1", "dp_2")
 DP_SEQ = ("dp_0", "dp_1", "dp_2", "seq")
 EPSILON = 1e-06
+
+
+def exchange_blocks(value, axis, split, join):
+    parts = jnp.split(value, lax.axis_size(axis), axis=split)
+    received = lax.all_to_all(jnp.stack(parts), axis, 0, 0)
+    return jnp.concatenate(received, axis=join)
 
 
 def copy_for_each(value, axis):
@@ -92,7 +98,7 @@
         jnp.arange(image_total, dtype=jnp.int32) - jnp.take(starts, owners)
     )
     outgoing = jnp.where(slot_live, jnp.take(own_cot, local_slots, axis=0), zero_half)
-    returned = lax.all_to_all(outgoing[None], "seq", split_axis=2, concat_axis=0, tiled=True)
+    returned = exchange_blocks(outgoing[None], "seq", 2, 0)
     image_cot = jnp.take(returned.reshape(-1, columns), flat_index, axis=0).astype(jnp.float32)
     emb_float = embedded.astype(jnp.float32)
     column_gain = lax.dynamic_slice_in_dim(norm_gain, seq_index * columns, columns)

time: 360 us -> 334 us (0.928)
  other arithmetic: 72.6 us -> 27.5 us
  waiting for transfers between devices: 104 us -> 141 us
  local copies, waits for them, and re-layouts: 47.6 us -> 29.4 us
    unnamed x2 -> x1, other arithmetic: 45.2 us -> 0.04 us
    all_gather x1, waiting for transfers between devices: 19.4 us -> 64.1 us  [on_device(): gathered = lax.all_gather(tile_tokens[0], 'seq', axis=0, tiled=True)]
    all_to_all x3 -> x0, local copies, waits for them, and re-layouts: 8.62 us -> none  [on_device(): lax.all_to_all(outgoing[None], 'seq', split_axis=2, concat_axis=0, tiled=...]
    all_to_all x1, waiting for transfers between devices: 36.3 us -> 28.3 us  [exchange_blocks(): received = lax.all_to_all(jnp.stack(parts), axis, 0, 0)]
    select_n x1 -> x0, local copies, waits for them, and re-layouts: 6.83 us -> none  [on_device(): jnp.where(slot_live, jnp.take(own_cot, local_slots, axis=0), zero_half)]
    unnamed x21 -> x32, local copies, waits for them, and re-layouts: 18.5 us -> 15.2 us
  transfers between devices with their start and end apart: 5 -> 5, of which waited for: 4 -> 4; matrix products, arithmetic and copies ran while one was open for 31% -> 14% of each run, Pallas kernels for 0% -> 0%
where the time goes in v1:
time: 334 us; the launch traced here: 333 us
  waiting for transfers between devices  141 us (42%)
  blocking collectives  88.4 us (26%)
  local copies, waits for them, and re-layouts  29.4 us (9%)
  other arithmetic  27.5 us (8%)
  starting transfers between devices  22.8 us (7%)
  between operations  14.7 us (4%)
  matrix products  9.25 us (3%)
    psum x4, blocking collectives, one_axis_at_a_time(): value = lax.psum(value, axis)  88.4 us
    all_gather x1, waiting for transfers between devices, on_device(): gathered = lax.all_gather(tile_tokens[0], 'seq', axis=0, tiled=True)  64.1 us
    unnamed x4, waiting for transfers between devices  38.3 us
    all_to_all x1, waiting for transfers between devices, exchange_blocks(): received = lax.all_to_all(jnp.stack(parts), axis, 0, 0)  28.3 us
    unnamed x32, local copies, waits for them, and re-layouts  15.2 us
    all_to_all x1, starting transfers between devices, exchange_blocks(): received = lax.all_to_all(jnp.stack(parts), axis, 0, 0)  15.2 us
    all_to_all x1, waiting for transfers between devices, copy_for_each(): return lax.all_to_all(copies, axis, split_axis=0, concat_axis=0, tiled=True)  10 us
    all_to_all x1, starting transfers between devices, copy_for_each(): return lax.all_to_all(copies, axis, split_axis=0, concat_axis=0, tiled=True)  7.51 us
  transfers between devices with their start and end apart: 5, of which 4 were waited for; matrix products, arithmetic and copies ran while one was open for 14% of the time, Pallas kernels for 0%

profile of v1, /device:TPU:6, one launch (start us, length us, event | category | flops | bytes accessed | tf_op | source)
XLA Modules:
  0.0 332.8 jit_solution(15616528988813262759)
XLA Ops:
  7.2 0.7 all-gather.7.cloned.1.call-update
  8.0 0.7 all-gather.5.cloned.1.call-update
  8.7 0.7 add_select_fusion
  10.3 0.7 fusion.55
  11.1 0.7 fusion.53
  11.8 1.5 gather_fusion
  13.3 0.7 fusion.52
  14.0 1.3 compare_and_fusion
  15.3 3.6 %gather_fusion.1 = bf16[48,8192]{1,0:T(8,128)(2,1)S(1)} fusion(bf16[128,8192]{1,0:T(8,128)(2,1)} %bitcast.145, s32[1024]{0:T(1024)S(1)} %pad_clamp_fusion.1), kind=kCustom, calls=%fused_computation.1 | custom fusion | bytes 1573056 | tf_op jit(solution)/shard_map/jit(_take)/gather | solution.py:100
  19.1 0.6 fusion.46
  19.7 0.6 fusion.45
  20.3 0.6 fusion.44
  21.0 0.6 fusion.43
  21.6 0.6 fusion.42
  22.2 0.6 fusion.41
  22.8 0.6 fusion.40
  25.3 0.6 fusion.36
  26.5 0.6 fusion.34
  27.1 0.6 fusion.33
  27.8 0.6 fusion.32
  28.4 0.6 fusion.31
  29.0 15.2 %all-to-all-start = ((bf16[16,1,48,512]{3,2,1,0:T(8,128)(2,1)}), bf16[16,1,48,512]{3,2,1,0:T(8,128)(2,1)S(1)}, u32[]{:S(2)}, u32[]{:S(2)}) async-start(bf16[16,1,48,512]{3,2,1,0:T(8,128)(2,1)} %fusion.31), calls=%async_computation | async-start | bytes 1572864 | tf_op jit(solution)/shard_map/all_to_all | solution.py:15
  44.2 0.8 dynamic_slice.14
  45.0 4.4 %compare_select_fusion.2 = (s32[512,1]{0,1:T(1,128)S(1)}, s32[512,1]{0,1:T(1,128)S(1)}, s32[512,1]{0,1:T(1,128)S(1)}, s32[512,1]{0,1:T(1,128)S(1)}) fusion(s32[]{:T(128)} %bitcast.12, s32[]{:T(128)} %bitcast.13, s32[]{:T(128)} %bitcast.14, s32[]{:T(128)} %bitcast.15, s32[]{:T(128)} %bitcast.16, s32[]{:T(128)} %bitcast.18, s32[]{:T(128)} %bitcast.17, ...), kind=kLoop, calls=%fused_computation.93 | loop fusion | flops 16384 | bytes 10268 | tf_op jit(solution)/shard_map/jit(_take)/gather | solution.py:98
  49.5 5.7 %compare_and_fusion.1 = (pred[512]{0:T(512)(128)(4,1)S(1)}, s32[512]{0:T(512)S(1)}) fusion(pred[512]{0:T(512)(128)(4,1)S(1)} %get-tuple-element.22, pred[512]{0:T(512)(128)(4,1)S(1)} %get-tuple-element.20, pred[512]{0:T(512)(128)(4,1)S(1)} %get-tuple-element.21, pred[512]{0:T(512)(128)(4,1)S(1)} %get-tuple-element.19, ...), kind=kLoop, calls=%fused_computation.133 | loop fusion | flops 20480 | bytes 11300 | tf_op jit(solution)/shard_map/jit(_take)/and | solution.py:102
  55.2 28.3 %all-to-all-done = bf16[16,1,48,512]{3,2,1,0:T(8,128)(2,1)S(1)} async-done(((bf16[16,1,48,512]{3,2,1,0:T(8,128)(2,1)}), bf16[16,1,48,512]{3,2,1,0:T(8,128)(2,1)S(1)}, u32[]{:S(2)}, u32[]{:S(2)}) %all-to-all-start) | async-done | bytes 786464 | tf_op jit(solution)/shard_map/all_to_all | solution.py:15
  83.5 2.0 gather_fusion.2
  85.5 1.0 copy.24
  86.5 3.7 %reshape.450 = bf16[3200,512]{1,0:T(8,128)(2,1)S(1)} reshape(bf16[32,100,512]{2,1,0:T(8,128)(2,1)} %all-gather.7.cloned.1.call-done) | data formatting | bytes 6553600
  90.3 64.1 %all-gather.5.cloned.1.call-done = bf16[1,512,3200]{2,1,0:T(8,128)(2,1)} async-done(((bf16[1,32,3200]{2,1,0:T(8,128)(2,1)}), bf16[1,512,3200]{2,1,0:T(8,128)(2,1)}) %all-gather.5.cloned.1.call-update) | async-done | bytes 3276816 | tf_op jit(solution)/shard_map/all_gather | solution.py:77
  154.4 4.9 %fusion.23 = (f32[512]{0:T(512)S(1)}, f32[512]{0:T(512)S(1)}, bf16[512,512]{0,1:T(8,128)(2,1)}) fusion(f32[512]{0:T(512)S(1)} %dynamic_slice.14, bf16[512,512]{0,1:T(8,128)(2,1)} %copy.24, pred[512]{0:T(512)(128)(4,1)S(1)} %get-tuple-element.23, bf16[3200,512]{1,0:T(8,128)(2,1)S(1)} %reshape.450, bf16[1,512,3200]{2,1,0:T(8,128)(2,1)} %all-gather.5.cloned.1.call-done), kind=kOutput, calls=%fused_computation.35 | convolution fusion | flops 1680079872 | bytes 7608832 | tf_op jit(solution)/shard_map/dot_general | solution.py:79
  159.3 0.7 broadcast_in_dim.90
  159.9 7.5 %all-to-all-start.1 = ((f32[16,1,1024]{2,1,0:T(1,128)}), f32[16,1,1024]{2,1,0:T(1,128)S(1)}, u32[]{:S(2)}, u32[]{:S(2)}) async-start(f32[16,1,1024]{2,1,0:T(1,128)} %broadcast_in_dim.90), calls=%async_computation.1 | async-start | bytes 131072 | tf_op jit(solution)/shard_map/all_to_all | solution.py:21
  167.6 2.6 scatter_custom_fusion
  170.2 10.0 %all-to-all-done.1 = f32[16,1,1024]{2,1,0:T(1,128)S(1)} async-done(((f32[16,1,1024]{2,1,0:T(1,128)}), f32[16,1,1024]{2,1,0:T(1,128)S(1)}, u32[]{:S(2)}, u32[]{:S(2)}) %all-to-all-start.1) | async-done | bytes 65568 | tf_op jit(solution)/shard_map/all_to_all | solution.py:21
  180.3 4.4 %multiply_reduce_fusion = (f32[3200]{0:T(1024)S(1)}, f32[512,3200]{1,0:T(8,128)S(1)}) fusion(bf16[1,512,3200]{2,1,0:T(8,128)(2,1)} %all-gather.5.cloned.1.call-done, bf16[512,512]{0,1:T(8,128)(2,1)} %get-tuple-element.48, f32[512]{0:T(512)S(1)} %get-tuple-element.29, f32[512]{0:T(512)S(1)} %get-tuple-element.28, f32[512]{0:T(512)S(1)} %dynamic_slice.14, ...), kind=kOutput, calls=%fused_computation.12 | convolution fusion | flops 1683354496 | bytes 10898432 | tf_op jit(solution)/shard_map/dot_general | solution.py:127
  184.8 6.4 %fusion.6 = bf16[3200,512]{0,1:T(8,128)(2,1)} fusion(f32[512,3200]{1,0:T(8,128)S(1)} %get-tuple-element.50, f32[3200]{0:T(1024)S(1)} %convert_reduce_fusion.1, f32[512]{0:T(512)S(1)} %bitcast.153, f32[3200]{0:T(1024)S(1)} %reduce.13, f32[3200]{0:T(1024)S(1)} %add_sqrt_fusion), kind=kLoop, calls=%fused_computation.13 | loop fusion | flops 29491200 | bytes 9870848 | tf_op jit(solution)/shard_map/convert_element_type | solution.py:131
  191.3 1.3 dynamic-slice.1
  193.3 2.1 fusion.10
  195.4 2.5 fusion.9
  198.4 14.1 %psum.28 = f32[8192]{0:T(1024)S(1)} all-reduce(f32[8192]{0:T(1024)S(1)} %add_dynamic-update-slice_fusion), channel_id=1, replica_groups=mesh['dp_0'=4,'dp_1'=4,'dp_2'=2,'seq'=16] {'dp_0'}, use_global_device_ids=true, to_apply=%region_11.12 | all-reduce | flops 8192 | bytes 65536 | tf_op jit(solution)/shard_map/psum | solution.py:40
  212.4 17.1 %psum.29 = f32[8192]{0:T(1024)S(1)} all-reduce(f32[8192]{0:T(1024)S(1)} %psum.28), channel_id=1, replica_groups=mesh['dp_0'=4,'dp_1'=4,'dp_2'=2,'seq'=16] {'dp_1'}, use_global_device_ids=true, to_apply=%region_12.13 | all-reduce | flops 8192 | bytes 65536 | tf_op jit(solution)/shard_map/psum | solution.py:40
  229.5 3.4 %psum.30 = f32[8192]{0:T(1024)S(1)} all-reduce(f32[8192]{0:T(1024)S(1)} %psum.29), channel_id=1, replica_groups=mesh['dp_0'=4,'dp_1'=4,'dp_2'=2,'seq'=16] {'dp_2'}, use_global_device_ids=true, to_apply=%region_13.14 | all-reduce | flops 8192 | bytes 65536 | tf_op jit(solution)/shard_map/psum | solution.py:40
  232.9 53.9 %psum.31 = f32[8192]{0:T(1024)S(1)} all-reduce(f32[8192]{0:T(1024)S(1)} %psum.30), channel_id=1, replica_groups=mesh['dp_0'=4,'dp_1'=4,'dp_2'=2,'seq'=16] {'seq'}, use_global_device_ids=true, to_apply=%region_14.15 | all-reduce | flops 8192 | bytes 65536 | tf_op jit(solution)/shard_map/psum | solution.py:40
  286.8 0.6 broadcast_multiply_fusion
  287.4 37.0 %all-reduce.3.cloned.1.call-done = bf16[3200,512]{0,1:T(8,128)(2,1)} async-done(((bf16[3200,512]{0,1:T(8,128)(2,1)}), bf16[3200,512]{0,1:T(8,128)(2,1)}) %all-reduce.3.cloned.1.call-update) | async-done | bytes 3276816
  324.4 1.1 convert_multiply_fusion.7
  325.4 0.8 copy.26
  (46 shorter events, 4.6 us)
Async XLA Ops:
  7.2 37.8 %copy-start = (s32[1,512]{1,0:T(1,128)S(1)}, s32[1,512]{1,0:T(1,128)}, u32[]{:S(2)}) copy-start(s32[1,512]{1,0:T(1,128)} %param.14) | copy-start | bytes 6148
  7.2 79.3 %all-gather.7.cloned.1.call-start = ((), (), s32[]{:S(2)}) async-start(), calls=%async_computation.3 | async-start | bytes 3514368 | tf_op jit(solution)/shard_map/all_gather | solution.py:81
  7.9 146.5 %all-gather.5.cloned.1.call-start = ((), (), s32[]{:S(2)}) async-start(), calls=%async_computation.2 | async-start | bytes 3481600 | tf_op jit(solution)/shard_map/all_gather | solution.py:77
  29.0 54.5 %all-to-all-start = ((bf16[16,1,48,512]{3,2,1,0:T(8,128)(2,1)}), bf16[16,1,48,512]{3,2,1,0:T(8,128)(2,1)S(1)}, u32[]{:S(2)}, u32[]{:S(2)}) async-start(bf16[16,1,48,512]{3,2,1,0:T(8,128)(2,1)} %fusion.31), calls=%async_computation | async-start | bytes 1572864 | tf_op jit(solution)/shard_map/all_to_all | solution.py:15
  90.2 77.2 %copy-start.5 = (f32[1,1,3200]{2,1,0:T(1,128)S(1)}, f32[1,1,3200]{2,1,0:T(1,128)}, u32[]{:S(2)}) copy-start(f32[1,1,3200]{2,1,0:T(1,128)} %param.16) | copy-start | bytes 38404
  90.3 79.9 %copy-start.4 = (s32[1,1,3200]{2,1,0:T(1,128)S(1)}, s32[1,1,3200]{2,1,0:T(1,128)}, u32[]{:S(2)}) copy-start(s32[1,1,3200]{2,1,0:T(1,128)} %param.15) | copy-start | bytes 38404
  159.2 25.5 %copy-start.6 = (f32[1,512]{1,0:T(1,128)S(1)}, f32[1,512]{1,0:T(1,128)}, u32[]{:S(2)}) copy-start(f32[1,512]{1,0:T(1,128)} %param.17) | copy-start | bytes 6148
  159.9 20.3 %all-to-all-start.1 = ((f32[16,1,1024]{2,1,0:T(1,128)}), f32[16,1,1024]{2,1,0:T(1,128)S(1)}, u32[]{:S(2)}, u32[]{:S(2)}) async-start(f32[16,1,1024]{2,1,0:T(1,128)} %broadcast_in_dim.90), calls=%async_computation.1 | async-start | bytes 131072 | tf_op jit(solution)/shard_map/all_to_all | solution.py:21
  167.4 156.9 %all-reduce.3.cloned.1.call-start = ((), (), s32[]{:S(2)}) async-start(), calls=%async_computation.4 | async-start | bytes 6553600
  184.8 10.6 %copy-start.1 = (bf16[1,128,8192]{2,1,0:T(8,128)(2,1)S(1)}, bf16[1,128,8192]{2,1,0:T(8,128)(2,1)}, u32[]{:S(2)}) copy-start(bf16[1,128,8192]{2,1,0:T(8,128)(2,1)} %param.12) | copy-start | bytes 6291460
  191.2 6.7 %copy-start.2 = (bf16[512,512]{0,1:T(8,128)(2,1)S(1)}, bf16[512,512]{0,1:T(8,128)(2,1)}, u32[]{:S(2)}) copy-start(bf16[512,512]{0,1:T(8,128)(2,1)} %copy.24) | copy-start | bytes 1572868
  191.2 6.7 %copy-start.3 = (bf16[512,512]{0,1:T(8,128)(2,1)S(1)}, bf16[512,512]{0,1:T(8,128)(2,1)}, u32[]{:S(2)}) copy-start(bf16[512,512]{0,1:T(8,128)(2,1)} %get-tuple-element.48) | copy-start | bytes 1572868
Sparse Core Ops, SparseCore 0:
  11.1 64.6 all-gather.6
  77.9 76.4 all-gather.4
  191.4 132.9 all-reduce.2
